TPU v7x, 256 devices: a whole 4x4x8 slice. The times are simulated.
256 devices in a mesh: seq: 16 (over x_lo, y, core), fsdp: 16 (over x_hi, z).
Axes of the slice: x: 4 (x_hi: 2, x_lo: 2; x = x_hi * 2 + x_lo), y: 4, z: 8, core: 2. Of those that a mesh axis runs over, the one named last changes fastest.
Arguments:
- tokens: bfloat16 [16, 2048, 4096], P('fsdp', 'seq'), may hold values from -6 to 6
- w_query: float32 [4096, 4096], P('fsdp', 'seq'), may hold values from -0.09375 to 0.09375
- w_key: float32 [4096, 4096], P('fsdp', 'seq'), may hold values from -0.09375 to 0.09375
- w_value: float32 [4096, 4096], P('fsdp', 'seq'), may hold values from -0.09375 to 0.09375
- short_taps: float32 [3, 3, 4096], P(None, None, 'seq'), may hold values from -4 to 4
- residue: float32 [4096, 16], P('seq'), may hold values from -11.35 to 11.35
- decay: float32 [4096, 16], P('seq'), may hold values from 0.00048828125 to 0.04
- passthrough: float32 [4096], P('seq'), may hold values from -4 to 4
Outputs:
- gated: bfloat16 [16, 2048, 4096], P('fsdp', 'seq')
All inputs are finite; a program needn't handle non-finite values.
Results may differ from a plain program's by a relative error of at most 0.0064.
Values may be sent and summed in bfloat16 or wider, within the bound.
A program may use at most 128 MiB of HBM per device.

v0:
```python
import jax
import jax.numpy as jnp
from jax import lax
from jax.sharding import PartitionSpec as P


def long_convolution(product, residue, decay):
    seq_len, channels = product.shape
    block_len = 128
    block_count = seq_len // block_len
    rates = decay.T
    mode_gain = residue.T * jnp.sqrt(rates)
    offsets = jnp.arange(block_len).astype(jnp.float32)
    short_filter = jnp.sum(mode_gain[None] * jnp.exp(-rates[None] * offsets[:, None, None]), axis=1)
    lag_grid = jnp.arange(block_len)[:, None] - jnp.arange(block_len)[None, :]
    toeplitz = jnp.where(
        (lag_grid >= 0)[:, :, None], short_filter[jnp.clip(lag_grid, 0, block_len - 1)], 0.0
    )
    pieces = product.reshape(block_count, block_len, channels)
    inner = jnp.einsum("ijc,bjc->bic", toeplitz, pieces, precision=lax.Precision.HIGHEST)
    entering = mode_gain[None] * jnp.exp(-rates[None] * (offsets[:, None, None] + 1.0))
    leaving = jnp.exp(-rates[None] * (block_len - 1.0 - offsets)[:, None, None])
    across = jnp.exp(-rates * block_len)

    def advance(carried, blocks):
        piece, local = blocks
        result = local + jnp.einsum(
            "irc,rc->ic", entering, carried, precision=lax.Precision.HIGHEST
        )
        carried = carried * across + jnp.einsum(
            "jrc,jc->rc", leaving, piece, precision=lax.Precision.HIGHEST
        )
        return (carried, result)

    start_state = jnp.zeros(rates.shape, jnp.float32)
    _, outputs = lax.scan(advance, start_state, (pieces, inner))
    return outputs.reshape(seq_len, channels)


def body(tokens, w_query, w_key, w_value, short_taps, residue, decay, passthrough):
    inputs = tokens[0]
    masters = jnp.concatenate(
        [w_query.astype(jnp.bfloat16), w_key.astype(jnp.bfloat16), w_value.astype(jnp.bfloat16)],
        axis=1,
    )
    channels = w_query.shape[1]
    weights = lax.all_gather(masters, "fsdp", axis=0, tiled=True)
    projected = jnp.dot(
        lax.all_gather(inputs, "seq", axis=0, tiled=True),
        weights,
        preferred_element_type=jnp.float32,
    )
    seq_len = projected.shape[0]
    stacked = jnp.transpose(projected.reshape(seq_len, 3, channels), (1, 0, 2))
    padded = jnp.pad(stacked, ((0, 0), (2, 0), (0, 0)))
    shorted = (
        short_taps[0][:, None, :] * stacked
        + short_taps[1][:, None, :] * padded[:, 1:-1]
        + short_taps[2][:, None, :] * padded[:, :-2]
    )
    product = shorted[1] * shorted[2]
    convolved = long_convolution(product, residue, decay)
    result = (shorted[0] * (convolved + passthrough[None, :] * product)).astype(jnp.bfloat16)
    back = lax.all_to_all(result, "seq", split_axis=0, concat_axis=1, tiled=True)
    return back[None]


def solution(mesh):
    return jax.shard_map(
        body,
        mesh=mesh,
        in_specs=(
            P("fsdp", "seq", None),
            P("fsdp", "seq"),
            P("fsdp", "seq"),
            P("fsdp", "seq"),
            P(None, None, "seq"),
            P("seq", None),
            P("seq", None),
            P("seq"),
        ),
        out_specs=P("fsdp", "seq", None),
        check_vma=False,
    )
```

profile of v0, /device:TPU:1, one launch (start us, length us, event | category | flops | bytes accessed | tf_op | source)
XLA Modules:
  0.0 368.4 jit_solution(6379386669887093202)
XLA Ops:
  11.8 61.7 %gather_fusion = f32[16384,256]{1,0:T(8,128)} fusion(f32[128,256]{1,0:T(8,128)S(1)} %multiply_reduce_fusion.2, s32[16384]{0:T(1024)S(1)} %fusion.18), kind=kCustom, calls=%fused_computation | custom fusion | bytes 33619968 | tf_op jit(solution)/shard_map/gather | solution.py:17
  73.4 18.0 %copy.23 = f32[128,128,256]{1,0,2:T(8,128)} copy(f32[128,128,256]{2,1,0:T(8,128)} %bitcast.66) | data formatting | bytes 33554432 | tf_op jit(solution)/shard_map/gather | solution.py:17
  91.5 37.6 %all-gather.4.cloned.1.call-done = bf16[4096,768]{1,0:T(8,128)(2,1)} async-done(((bf16[256,768]{1,0:T(8,128)(2,1)}), bf16[4096,768]{1,0:T(8,128)(2,1)}) %all-gather.4.cloned.1.call-update) | async-done | bytes 6291472 | tf_op jit(solution)/shard_map/all_gather | solution.py:47
  129.1 94.3 %all-gather.6.cloned.1.call-done = bf16[1,2048,4096]{2,1,0:T(8,128)(2,1)} async-done(((bf16[1,128,4096]{2,1,0:T(8,128)(2,1)}), bf16[1,2048,4096]{2,1,0:T(8,128)(2,1)}) %all-gather.6.cloned.1.call-update) | async-done | bytes 16777232 | tf_op jit(solution)/shard_map/all_gather | solution.py:49
  223.4 17.9 %fusion.4 = f32[768,2048]{1,0:T(8,128)S(1)} fusion(bf16[4096,768]{1,0:T(8,128)(2,1)} %all-gather.4.cloned.1.call-done, bf16[1,2048,4096]{2,1,0:T(8,128)(2,1)} %all-gather.6.cloned.1.call-done), kind=kOutput, calls=%fused_computation.11 | convolution fusion | flops 12884901888 | bytes 29360128 | tf_op jit(solution)/shard_map/dot_general | solution.py:48
  241.4 4.6 %fusion.12 = f32[3,2048,256]{1,2,0:T(8,128)S(1)} fusion(f32[3,2048,256]{1,2,0:T(8,128)S(1)} %bitcast.70, f32[3,256]{1,0:T(4,128)S(1)} %get-tuple-element.201, f32[3,256]{1,0:T(4,128)S(1)} %get-tuple-element.202, f32[3,256]{1,0:T(4,128)S(1)} %get-tuple-element.200), kind=kLoop, calls=%fused_computation.21 | loop fusion | flops 7864320 | bytes 12592128 | tf_op jit(solution)/shard_map/add | solution.py:57
  245.9 2.5 slice_multiply_fusion
  248.5 1.9 copy.22
  250.4 2.0 copy.24
  252.4 29.5 %fusion.14 = f32[16,128,256]{1,0,2:T(8,128)} fusion(f32[16,128,256]{1,0,2:T(8,128)} %copy.24, f32[128,128,256]{1,0,2:T(8,128)} %copy.23, pred[128,128]{1,0:T(8,128)(4,1)S(1)} %subtract_compare_fusion), kind=kOutput, calls=%fused_computation.26 | convolution fusion | flops 809500672 | bytes 20987904 | tf_op jit(solution)/shard_map/ijc,bjc->bic/dot_general | solution.py:20
  281.9 51.9 %while.15 = (s32[]{:T(128)}, f32[16,256]{1,0:T(8,128)S(1)}, f32[16,128,256]{2,1,0:T(8,128)}, f32[16,256]{1,0:T(8,128)S(1)}, f32[16,128,256]{2,1,0:T(8,128)S(1)},...) while((s32[]{:T(128)}, f32[16,256]{1,0:T(8,128)S(1)}, ...), condition=%wide.region_2.3_spmd.clone.clone.clone, body=%wide.region_1.2_spmd.clone.clone.clone.sunk | while | flops 3678211 | bytes 1607303 | solution.py:36
  289.6 1.3 constant_dynamic-slice_fusion.2
  292.8 1.3 constant_dynamic-slice_fusion.2
  296.1 1.3 constant_dynamic-slice_fusion.2
  299.3 1.3 constant_dynamic-slice_fusion.2
  305.8 1.3 constant_dynamic-slice_fusion.2
  309.0 1.3 constant_dynamic-slice_fusion.2
  312.3 1.3 constant_dynamic-slice_fusion.2
  315.5 1.3 constant_dynamic-slice_fusion.2
  318.8 1.3 constant_dynamic-slice_fusion.2
  322.0 1.3 constant_dynamic-slice_fusion.2
  333.8 3.0 copy.21
  336.7 2.7 multiply_convert_fusion
  339.5 20.2 %all_to_all.13 = bf16[16,128,256]{2,1,0:T(8,128)(2,1)S(1)} all-to-all(bf16[16,128,256]{2,1,0:T(8,128)(2,1)S(1)} %multiply_convert_fusion), channel_id=1, replica_groups=mesh['seq'=16,'fsdp'=16] {'seq'}, dimensions={0} | all-to-all | bytes 2097152 | tf_op jit(solution)/shard_map/all_to_all | solution.py:64
  (130 shorter events, 45.0 us)
Async XLA Ops:
  6.5 4.5 %copy-start.1 = (f32[256,16]{0,1:T(8,128)S(1)}, f32[256,16]{0,1:T(8,128)}, u32[]{:S(2)}) copy-start(f32[256,16]{0,1:T(8,128)} %param.15) | copy-start | bytes 49156
  6.5 4.5 %copy-start = (f32[256,16]{0,1:T(8,128)S(1)}, f32[256,16]{0,1:T(8,128)}, u32[]{:S(2)}) copy-start(f32[256,16]{0,1:T(8,128)} %param.16) | copy-start | bytes 49156
  6.5 122.6 %all-gather.4.cloned.1.call-start = ((), (), s32[]{:S(2)}) async-start(), calls=%async_computation.1 | async-start | bytes 6684672 | tf_op jit(solution)/shard_map/all_gather | solution.py:47
  10.3 213.1 %all-gather.6.cloned.1.call-start = ((), (), s32[]{:S(2)}) async-start(), calls=%async_computation.2 | async-start | bytes 17825792 | tf_op jit(solution)/shard_map/all_gather | solution.py:49
  73.4 18.0 %copy-start.2 = (f32[3,3,256]{2,1,0:T(4,128)S(1)}, f32[3,3,256]{2,1,0:T(4,128)}, u32[]{:S(2)}) copy-start(f32[3,3,256]{2,1,0:T(4,128)} %param.14) | copy-start | bytes 27652
  333.8 3.0 copy-start.3
Sparse Core Ops, SparseCore 0:
  10.4 118.6 all-gather.3
  131.0 92.4 all-gather.5
where the time goes:
time: 370 us; the launch traced here: 368 us
  waiting for transfers between devices  133 us (36%)
  local copies, waits for them, and re-layouts  111 us (30%)
  matrix products  47.5 us (13%)
  other arithmetic  42.6 us (12%)
  blocking collectives  20.2 us (5%)
  between operations  13.5 us (4%)
    all_gather x1, waiting for transfers between devices, body(): lax.all_gather(inputs, 'seq', axis=0, tiled=True)  94.3 us
    gather x2, local copies, waits for them, and re-layouts, long_convolution(): short_filter[jnp.clip(lag_grid, 0, block_len - 1)]  79.7 us
    all_gather x1, waiting for transfers between devices, body(): weights = lax.all_gather(masters, 'fsdp', axis=0, tiled=True)  37.6 us
    dot_general x1, matrix products, long_convolution(): jnp.einsum('ijc,bjc->bic', toeplitz, pieces, precision=lax.Precision.HIGH...  29.5 us
    dynamic_slice x32, local copies, waits for them, and re-layouts, long_convolution(): _, outputs = lax.scan(advance, start_state, (pieces, inner))  22.7 us
    all_to_all x1, blocking collectives, body(): lax.all_to_all(result, 'seq', split_axis=0, concat_axis=1, tiled=True)  20.2 us
    dot_general x1, matrix products, body(): jnp.dot(lax.all_gather(inputs, 'seq', axis=0, tiled=True), weights, prefe...  17.9 us
    dot_general x16, other arithmetic, advance(): jnp.einsum('irc,rc->ic', entering, carried, precision=lax.Precision.HIGHEST)  10.9 us
  transfers between devices with their start and end apart: 2, of which 2 were waited for; matrix products, arithmetic and copies ran while one was open for 22% of the time, Pallas kernels for 0%

commit v1 on v0

v1 whole, which is shorter than its diff:
```python
import functools
import jax, jax.numpy as jnp
from jax import lax
from jax.experimental import pallas as pl
from jax.experimental.pallas import tpu as pltpu
from jax.sharding import PartitionSpec as P

MODES = 16
PITCH = 264

def shift_rows(v, n, row):
    return jnp.where(row >= n, pltpu.roll(v, n, 0), 0.0)

def conv_half(acc, prod, res, taps, rates, gains, skip, unroll1=8, unroll2=8, chunk=None, emit=None):
    segs, span = 8, 256
    row = lax.broadcasted_iota(jnp.int32, (segs, 128), 0)
    wide = lambda v: jnp.broadcast_to(v, (segs, 128))
    fade = [wide(jnp.exp(-rates[r:r + 1])) for r in range(MODES)]
    def at(t, j):
        return acc[j, pl.ds(t, segs, stride=PITCH), :]
    def first(j):
        return shift_rows(at(span - 1, j), 1, row), shift_rows(at(span - 2, j), 1, row)
    tk = [wide(taps(i, 1)) for i in range(3)]
    tv = [wide(taps(i, 2)) for i in range(3)]
    def step1(t, c):
        k1, k2, v1, v2, hs = c
        k, v = at(t, 1), at(t, 2)
        p = (tk[0] * k + tk[1] * k1 + tk[2] * k2) * (tv[0] * v + tv[1] * v1 + tv[2] * v2)
        prod[pl.ds(pl.multiple_of(t * segs, segs), segs), :] = p
        return k, k1, v, v1, tuple(fade[r] * hs[r] + p for r in range(MODES))
    zero = jnp.zeros((segs, 128), jnp.float32)
    k1, k2 = first(1); v1, v2 = first(2)
    *_, hs = lax.fori_loop(0, span, step1, (k1, k2, v1, v2, (zero,) * MODES), unroll=unroll1)
    start = []
    for r in range(MODES):
        h = hs[r]
        for n in (1, 2, 4):
            h = h + wide(jnp.exp(-rates[r:r + 1] * float(span * n))) * shift_rows(h, n, row)
        start.append(shift_rows(h, 1, row))
    tq = [wide(taps(i, 0)) for i in range(3)]
    gain = [wide(gains[r:r + 1]) for r in range(MODES)]
    thru = wide(skip)
    def step2(t, c):
        q1, q2, hs = c
        q = at(t, 0)
        p = prod[pl.ds(pl.multiple_of(t * segs, segs), segs), :]
        hs = tuple(fade[r] * hs[r] + p for r in range(MODES))
        parts = [gain[r] * hs[r] for r in range(MODES)] + [thru * p]
        while len(parts) > 1:
            parts = [a + b for a, b in zip(parts[::2], parts[1::2])] + ([parts[-1]] if len(parts) % 2 else [])
        res[pl.ds(t, segs, stride=PITCH), :] = (tq[0] * q + tq[1] * q1 + tq[2] * q2) * parts[0]
        return q, q1, hs
    q1, q2 = first(0)
    c = (q1, q2, tuple(start))
    c = lax.fori_loop(0, span // 2, step2, c, unroll=unroll2)
    if emit: emit(0)
    c = lax.fori_loop(span // 2, span, step2, c, unroll=unroll2)
    if emit: emit(1)

def kernel(u1, u2, proj, taps, rates, residue, skip, out, prod, res, acc):
    def load(i, _):
        rows = pl.ds(pl.multiple_of(i * 256, 256), 256)
        for j in range(3):
            acc[j, pl.ds(pl.multiple_of(i * PITCH, 8), 256), :] = proj[rows, 128 * j:128 * j + 128]
        return 0
    lax.fori_loop(0, 8, load, 0)
    rt = rates[...]
    gains = residue[...] * jnp.sqrt(rt)
    conv_half(acc, prod, res, lambda i, j: taps[i, j:j + 1, :], rt, gains, skip[...], u1, u2)
    def cast(i, _):
        rows = pl.ds(pl.multiple_of(i * 256, 256), 256)
        out[rows, :] = res[pl.ds(pl.multiple_of(i * PITCH, 8), 256), :].astype(jnp.bfloat16)
        return 0
    lax.fori_loop(0, 8, cast, 0)

def conv(projected, short_taps, rates_t, residue_t, skip, u1=8, u2=8):
    return pl.pallas_call(functools.partial(kernel, u1, u2),
        grid=(2,),
        out_shape=jax.ShapeDtypeStruct((2048, 256), jnp.bfloat16),
        in_specs=[pl.BlockSpec((2048, 384), lambda h: (0, h)), pl.BlockSpec((3, 3, 128), lambda h: (0, 0, h)),
                  pl.BlockSpec((16, 128), lambda h: (0, h)), pl.BlockSpec((16, 128), lambda h: (0, h)), pl.BlockSpec((1, 128), lambda h: (0, h))],
        out_specs=pl.BlockSpec((2048, 128), lambda h: (0, h)),
        scratch_shapes=[pltpu.VMEM((2048, 128), jnp.float32), pltpu.VMEM((8 * PITCH, 128), jnp.float32)] + [pltpu.VMEM((3, 8 * PITCH, 128), jnp.float32)],
        compiler_params=pltpu.CompilerParams(vmem_limit_bytes=40 << 20),
    )(projected, short_taps, rates_t, residue_t, skip)


def body(tokens, w_query, w_key, w_value, short_taps, residue, decay, passthrough):
    masters = [w.astype(jnp.bfloat16) for w in (w_query, w_key, w_value)]
    masters = jnp.concatenate([w[:, h:h + 128] for h in (0, 128) for w in masters], axis=1)
    weights = lax.all_gather(masters, "fsdp", axis=0, tiled=True)
    inputs = lax.all_gather(tokens[0], "seq", axis=0, tiled=True)
    projected = jnp.dot(inputs, weights, preferred_element_type=jnp.float32)
    result = conv(projected, short_taps, decay.T, residue.T, passthrough[None])
    return lax.all_to_all(result, "seq", split_axis=0, concat_axis=1, tiled=True)[None]


def solution(mesh):
    return jax.shard_map(
        body,
        mesh=mesh,
        in_specs=(
            P("fsdp", "seq", None),
            P("fsdp", "seq"),
            P("fsdp", "seq"),
            P("fsdp", "seq"),
            P(None, None, "seq"),
            P("seq", None),
            P("seq", None),
            P("seq"),
        ),
        out_specs=P("fsdp", "seq", None),
        check_vma=False,
    )
```

time: 370 us -> 282 us (0.76)
  local copies, waits for them, and re-layouts: 111 us -> 2.77 us
  waiting for transfers between devices: 133 us -> 213 us
  other arithmetic: 42.6 us -> 2.9 us
  matrix products: 47.5 us -> 18.2 us
  Pallas kernels: 0 us -> 11.2 us
    all_gather x1, waiting for transfers between devices: 37.6 us -> 118 us  [body(): weights = lax.all_gather(masters, 'fsdp', axis=0, tiled=True)]
    gather x2 -> x0, local copies, waits for them, and re-layouts: 79.7 us -> none  [long_convolution(): short_filter[jnp.clip(lag_grid, 0, block_len - 1)]]
    dot_general x2 -> x1, matrix products: 47.5 us -> 18.2 us  [body(): projected = jnp.dot(inputs, weights, preferred_element_type=jnp.float32)]
    dynamic_slice x32 -> x0, local copies, waits for them, and re-layouts: 22.7 us -> none  [long_convolution(): _, outputs = lax.scan(advance, start_state, (pieces, inner))]
    dot_general x32 -> x0, other arithmetic: 17.5 us -> none  [the longest x16 10.9 us: advance(): jnp.einsum('irc,rc->ic', entering, carried, precision=lax.Precision.HIGHEST)]
    pallas_call x0 -> x1, Pallas kernels: none -> 11.2 us  [conv(): pl.pallas_call(functools.partial(kernel, u1, u2), grid=(2,), out_shape=ja...]
    dynamic_update_slice x16 -> x0, other arithmetic: 10.7 us -> none  [long_convolution(): _, outputs = lax.scan(advance, start_state, (pieces, inner))]
    add x2 -> x0, other arithmetic: 4.56 us -> none  [the longest x1 4.55 us: body(): short_taps[0][:, None, :] * stacked]
  transfers between devices with their start and end apart: 2 -> 2, of which waited for: 2 -> 2; matrix products, arithmetic and copies ran while one was open for 22% -> 0% of each run, Pallas kernels for 0% -> 0%
where the time goes in v1:
time: 282 us
  waiting for transfers between devices  213 us (76%)
  blocking collectives  20.2 us (7%)
  matrix products  18.2 us (6%)
  between operations  13.5 us (5%)
  Pallas kernels  11.2 us (4%)
  other arithmetic  2.9 us (1%)
    all_gather x1, waiting for transfers between devices, body(): weights = lax.all_gather(masters, 'fsdp', axis=0, tiled=True)  118 us
    all_gather x1, waiting for transfers between devices, body(): inputs = lax.all_gather(tokens[0], 'seq', axis=0, tiled=True)  94.3 us
    all_to_all x1, blocking collectives, body(): lax.all_to_all(result, 'seq', split_axis=0, concat_axis=1, tiled=True)[None]  20.2 us
    dot_general x1, matrix products, body(): projected = jnp.dot(inputs, weights, preferred_element_type=jnp.float32)  18.2 us
    pallas_call x1, Pallas kernels, conv(): pl.pallas_call(functools.partial(kernel, u1, u2), grid=(2,), out_shape=ja...  11.2 us
  transfers between devices with their start and end apart: 2, of which 2 were waited for; matrix products, arithmetic and copies ran while one was open for 0% of the time, Pallas kernels for 0%

profile of v1, /device:TPU:1, one launch (start us, length us, event | category | flops | bytes accessed | tf_op | source)
XLA Modules:
  0.0 281.9 jit_solution(5383643226657833497)
XLA Ops:
  6.5 0.0 all-gather.4.cloned.1.call-start
  6.5 1.0 convert_element_type.9
  7.5 1.0 convert_element_type.10
  8.5 1.0 convert_element_type.11
  9.6 0.0 copy-start.4
  9.6 0.7 copy-done.4
  10.3 0.0 all-gather.4.cloned.1.call-update
  10.4 0.0 all-gather.6.cloned.1.call-start
  10.4 0.7 all-gather.6.cloned.1.call-update
  11.1 0.0 copy-start
  11.1 0.0 copy-start.1
  11.1 0.0 copy-start.2
  11.2 0.0 copy-start.3
  11.2 118.0 %all-gather.4.cloned.1.call-done = bf16[4096,768]{1,0:T(8,128)(2,1)} async-done(((bf16[256,768]{1,0:T(8,128)(2,1)}), bf16[4096,768]{1,0:T(8,128)(2,1)}) %all-gather.4.cloned.1.call-update) | async-done | bytes 6291472 | tf_op jit(solution)/shard_map/all_gather | solution.py:91
  129.2 94.3 %all-gather.6.cloned.1.call-done = bf16[1,2048,4096]{2,1,0:T(8,128)(2,1)} async-done(((bf16[1,128,4096]{2,1,0:T(8,128)(2,1)}), bf16[1,2048,4096]{2,1,0:T(8,128)(2,1)}) %all-gather.6.cloned.1.call-update) | async-done | bytes 16777232 | tf_op jit(solution)/shard_map/all_gather | solution.py:92
  223.5 18.2 %fusion.2.proj = f32[2048,768]{1,0:T(8,128)S(1)} fusion(bf16[4096,768]{1,0:T(8,128)(2,1)} %all-gather.4.cloned.1.call-done, bf16[1,2048,4096]{2,1,0:T(8,128)(2,1)} %all-gather.6.cloned.1.call-done), kind=kOutput, calls=%fused_computation.2 | convolution fusion | flops 12884901888 | bytes 29360128 | tf_op jit(solution)/shard_map/dot_general | solution.py:93
  241.7 0.0 copy-done
  241.7 0.0 copy-done.1
  241.7 0.0 copy-done.2
  241.7 0.0 copy-done.3
  241.7 11.2 %shard_map.82 = bf16[2048,256]{1,0:T(8,128)(2,1)S(1)} custom-call(f32[2048,768]{1,0:T(8,128)S(1)} %fusion.2.proj, f32[3,3,256]{2,1,0:T(4,128)S(1)} %copy-done.2, f32[16,256]{1,0:T(8,128)S(1)} %bitcast.14, f32[16,256]{1,0:T(8,128)S(1)} %bitcast.15, f32[1,256]{1,0:T(1,128)S(1)} %bitcast.16), custom_call_target="tpu_custom_call" | custom-call | tf_op jit(solution)/shard_map/pallas_call | solution.py:77
  253.0 20.2 %all_to_all.16 = bf16[16,128,256]{2,1,0:T(8,128)(2,1)S(1)} all-to-all(bf16[16,128,256]{2,1,0:T(8,128)(2,1)S(1)} %bitcast.13), channel_id=1, replica_groups=mesh['seq'=16,'fsdp'=16] {'seq'}, dimensions={0} | all-to-all | bytes 2097152 | tf_op jit(solution)/shard_map/all_to_all | solution.py:95
  273.2 0.6 copy.10
  273.8 1.3 broadcast_in_dim.7
  (6 shorter events, 0.1 us)
Async XLA Ops:
  6.5 122.7 %all-gather.4.cloned.1.call-start = ((), (), s32[]{:S(2)}) async-start(), calls=%async_computation.1 | async-start | bytes 6684672 | tf_op jit(solution)/shard_map/all_gather | solution.py:91
  9.6 0.7 copy-start.4
  10.4 213.1 %all-gather.6.cloned.1.call-start = ((), (), s32[]{:S(2)}) async-start(), calls=%async_computation.2 | async-start | bytes 17825792 | tf_op jit(solution)/shard_map/all_gather | solution.py:92
  11.1 230.6 %copy-start = (f32[256,16]{0,1:T(8,128)S(1)}, f32[256,16]{0,1:T(8,128)}, u32[]{:S(2)}) copy-start(f32[256,16]{0,1:T(8,128)} %param.14) | copy-start | bytes 49156
  11.1 230.6 %copy-start.1 = (f32[256,16]{0,1:T(8,128)S(1)}, f32[256,16]{0,1:T(8,128)}, u32[]{:S(2)}) copy-start(f32[256,16]{0,1:T(8,128)} %param.13) | copy-start | bytes 49156
  11.1 230.6 %copy-start.2 = (f32[3,3,256]{2,1,0:T(4,128)S(1)}, f32[3,3,256]{2,1,0:T(4,128)}, u32[]{:S(2)}) copy-start(f32[3,3,256]{2,1,0:T(4,128)} %taps.1) | copy-start | bytes 27652
  11.2 230.6 %copy-start.3 = (f32[256]{0:T(256)S(1)}, f32[256]{0:T(256)}, u32[]{:S(2)}) copy-start(f32[256]{0:T(256)} %param.15) | copy-start | bytes 3076
Sparse Core Ops, SparseCore 0:
  10.5 118.6 all-gather.3
  131.0 92.4 all-gather.5

commit v2 on v1

v2 whole, which is shorter than its diff:
```python
import functools

import jax
import jax.numpy as jnp
from jax import lax
from jax.experimental import pallas as pl
from jax.experimental.pallas import tpu as pltpu
from jax.sharding import PartitionSpec as P

MESH = pl.DeviceIdType.MESH
MODES = 16
SEGS, SPAN = 8, 256
PITCH = 264
SPLIT = 9 * 256
HALVES = (0, 1)

UP = [("o", 0, 0), ("o", 0, 1), ("o", 1, 0), ("p", 0, 0), ("o", 2, 0), ("p", 1, 0), ("o", 3, 0), ("p", 2, 0),
      ("o", 1, 1), ("p", 0, 1), ("o", 2, 1), ("p", 1, 1), ("o", 3, 1), ("p", 2, 1)]
DOWN = [("o", 0, 0), ("o", 0, 1), ("p", 0, 0), ("o", 1, 0), ("p", 1, 0), ("o", 2, 0), ("p", 2, 0), ("p", 0, 1),
        ("p", 3, 0), ("p", 1, 1), ("o", 1, 1), ("p", 2, 1), ("o", 2, 1), ("p", 3, 1)]

PIECES = {
    "AX": ("A", 1, 0, None), "AU": ("A", 0, 1, None), "AD": ("A", 0, 3, None), "AXU": ("A", 1, 1, None), "AXD": ("A", 1, 3, None),
    "AO0": ("A", 0, 2, 0), "AO1": ("A", 0, 2, 1), "AXO0": ("A", 1, 2, 0), "AXO1": ("A", 1, 2, 1),
    "BX": ("B", 1, 0, None), "BU": ("B", 0, 1, None), "BD": ("B", 0, 3, None), "BXU": ("B", 1, 1, None), "BXD": ("B", 1, 3, None),
    "BO0": ("B", 0, 2, 0), "BO1": ("B", 0, 2, 1), "BXO0": ("B", 1, 2, 0), "BXO1": ("B", 1, 2, 1),
}
NAMES = list(PIECES)


def shift_rows(v, n, row):
    return jnp.where(row >= n, pltpu.roll(v, n, 0), 0.0)


def conv_half(half, acc, prod, res, taps, rates, gains, skip, emit):
    row = lax.broadcasted_iota(jnp.int32, (SEGS, 128), 0)
    wide = lambda v: jnp.broadcast_to(v, (SEGS, 128))
    fade = [wide(jnp.exp(-rates[r:r + 1])) for r in range(MODES)]

    def at(t, j):
        return acc[3 * half + j, pl.ds(t, SEGS, stride=PITCH), :]

    def before(j):
        return shift_rows(at(SPAN - 1, j), 1, row), shift_rows(at(SPAN - 2, j), 1, row)

    tap = [[wide(taps[i, j:j + 1, half * 128:half * 128 + 128]) for i in range(3)] for j in range(3)]

    def first(t, carry):
        k1, k2, v1, v2, hs = carry
        k, v = at(t, 1), at(t, 2)
        p = (tap[1][0] * k + tap[1][1] * k1 + tap[1][2] * k2) * (tap[2][0] * v + tap[2][1] * v1 + tap[2][2] * v2)
        prod[pl.ds(pl.multiple_of(t * SEGS, SEGS), SEGS), :] = p
        return k, k1, v, v1, tuple(fade[r] * hs[r] + p for r in range(MODES))

    zero = jnp.zeros((SEGS, 128), jnp.float32)
    *_, hs = lax.fori_loop(0, SPAN, first, (*before(1), *before(2), (zero,) * MODES), unroll=8)
    start = []
    for r in range(MODES):
        h = hs[r]
        for n in (1, 2, 4):
            h = h + wide(jnp.exp(-rates[r:r + 1] * float(SPAN * n))) * shift_rows(h, n, row)
        start.append(shift_rows(h, 1, row))
    gain = [wide(gains[r:r + 1]) for r in range(MODES)]
    thru = wide(skip)

    def second(t, carry):
        q1, q2, hs = carry
        q = at(t, 0)
        p = prod[pl.ds(pl.multiple_of(t * SEGS, SEGS), SEGS), :]
        hs = tuple(fade[r] * hs[r] + p for r in range(MODES))
        parts = [gain[r] * hs[r] for r in range(MODES)] + [thru * p]
        while len(parts) > 1:
            parts = [a + b for a, b in zip(parts[::2], parts[1::2])] + ([parts[-1]] if len(parts) % 2 else [])
        res[pl.ds(t, SEGS, stride=PITCH), :] = (tap[0][0] * q + tap[0][1] * q1 + tap[0][2] * q2) * parts[0]
        return q, q1, hs

    carry = (*before(0), tuple(start))
    for core in range(2):
        carry = lax.fori_loop(core * (SPAN // 2), (core + 1) * (SPAN // 2), second, carry, unroll=8)
        emit(core)


def kernel(tokens, w_query, w_key, w_value, taps, residue, decay, skip, out,
           tok, wts, masters, acc, prod, res, stage,
           load_sem, z_send, z_recv, h_send, h_recv, t_send, t_recv, d_send, d_recv, o_send, o_recv, o_local):
    s, f = lax.axis_index("seq"), lax.axis_index("fsdp")
    xl, y, c = s // 8, (s // 2) % 4, s % 2
    xh, z = f // 8, f % 8

    def seg(dx, dy):
        return ((xl + dx) % 2) * 4 + (y + dy) % 4

    def dev(dx, dy, core):
        return (seg(dx, dy) * 2 + core, f)

    def nth(n):
        return n // 4, n % 4

    z_dev = [(s, xh * 8 + (z + 1) % 8), (s, xh * 8 + (z + 7) % 8)]
    h_dev = (s, (1 - xh) * 8 + z)
    sib = dev(0, 0, 1 - c)
    sends = []

    barrier = pltpu.get_barrier_semaphore()

    def greet(n, _):
        for core in range(2):
            pl.semaphore_signal(barrier, inc=1, device_id=dev(*nth(n), core), device_id_type=MESH)
        return 0

    lax.fori_loop(1, 8, greet, 0)
    for d in (*z_dev, h_dev, sib):
        pl.semaphore_signal(barrier, inc=1, device_id=d, device_id_type=MESH)

    def own_rows(core, half=None):
        start = (seg(0, 0) * 2 + core) * 128
        return pl.ds(pl.multiple_of(start, 128), 128)

    loads = [pltpu.make_async_copy(w, masters.at[j], load_sem.at[j]) for j, w in enumerate((w_query, w_key, w_value))]
    loads.append(pltpu.make_async_copy(tokens.at[0], tok.at[own_rows(c), :], load_sem.at[3]))
    for load in loads:
        load.start()
    for load in loads[:3]:
        load.wait()
    mine = pl.ds(pl.multiple_of(f * 256, 256), 256)
    for h in HALVES:
        for j in range(3):
            wts[h, mine, 128 * j:128 * j + 128] = masters[j, :, 128 * h:128 * h + 128].astype(jnp.bfloat16)
    rates = decay[...].T
    gains = residue[...].T * jnp.sqrt(rates)
    loads[3].wait()
    pl.semaphore_wait(barrier, 18)

    def t_ref(part, dx, dy, rows, core):
        start = (seg(dx, dy) * 2 + core) * 128 + (0 if rows is None else 64 * rows)
        rows = pl.ds(pl.multiple_of(start, 64), 128 if rows is None else 64)
        return tok.at[rows, pl.ds(0, SPLIT) if part == "A" else pl.ds(SPLIT, 4096 - SPLIT)]

    def remote(src, dst, send, recv, device):
        return pltpu.make_async_remote_copy(src_ref=src, dst_ref=dst, send_sem=send, recv_sem=recv, device_id=device, device_id_type=MESH)

    def push(part, dx, dy, rows, device, name):
        ref, n = t_ref(part, dx, dy, rows, c), NAMES.index(name)
        copy = remote(ref, ref, t_send.at[n], t_recv.at[n], device)
        copy.start()
        sends.append(copy)

    def share(n, ref):
        copy = remote(ref, ref, d_send.at[n], d_recv.at[n], sib)
        copy.start()
        sends.append(copy)

    here, shared = set(), set()

    def arrive(*names):
        for name in names:
            n, ref = NAMES.index(name), t_ref(*PIECES[name], c)
            remote(ref, ref, t_send.at[n], t_recv.at[n], sib).wait_recv()
            share(n, ref)
            here.add(name)

    def other(*names):
        for name in names:
            n, ref = NAMES.index(name), t_ref(*PIECES[name], 1 - c)
            remote(ref, ref, d_send.at[n], d_recv.at[n], sib).wait_recv()
            shared.add(name)

    up, down, across = dev(0, 1, c), dev(0, 3, c), dev(1, 0, c)
    push("A", 0, 0, None, across, "AX")
    push("B", 0, 0, None, up, "BD")
    push("B", 0, 0, None, down, "BU")

    def w_ref(h, kind, steps):
        block = (xh if kind == "o" else 1 - xh) * 8 + (z + steps) % 8
        return wts.at[h, pl.ds(pl.multiple_of(block * 256, 256), 256), :]

    hop = [remote(w_ref(h, "o", 0), w_ref(h, "o", 0), h_send.at[h], h_recv.at[h], h_dev) for h in HALVES]
    sends.extend(hop)
    arrived = {("o", 0, 0), ("o", 0, 1)}

    def place(way, kind, far):
        return 8 - far if way == 0 else far

    def w_arrive(way, kind, far, h):
        key = (kind, far if way else -far, h)
        if key in arrived:
            return
        if far == 0:
            ref = w_ref(h, "p", 0)
            remote(ref, ref, h_send.at[h], h_recv.at[h], h_dev).wait_recv()
        else:
            n = (UP, DOWN)[way].index((kind, far - 1, h))
            ref = w_ref(h, kind, place(way, kind, far))
            remote(ref, ref, z_send.at[way, n], z_recv.at[way, n], z_dev[way]).wait_recv()
        arrived.add(key)

    def z_step(n):
        for way in range(2):
            kind, far, h = (UP, DOWN)[way][n]
            w_arrive(way, kind, far, h)
            ref = w_ref(h, kind, place(way, kind, far))
            copy = remote(ref, ref, z_send.at[way, n], z_recv.at[way, n], z_dev[way])
            copy.start()
            sends.append(copy)

    hop[0].start()
    z_step(0)
    push("A", 0, 0, None, up, "AD")
    push("A", 0, 0, None, down, "AU")
    push("B", 0, 0, None, across, "BX")
    z_step(1)
    hop[1].start()
    own = tok.at[own_rows(c), :]
    share(len(NAMES), own)

    def rows_of(g):
        return pl.ds(pl.multiple_of(g * SPAN, SPAN), SPAN), pl.ds(pl.multiple_of(g * PITCH, 8), SPAN)

    def whole(h, g):
        src, dst = rows_of(g)
        r = jnp.dot(tok[src, :], wts[h], preferred_element_type=jnp.float32)
        for j in range(3):
            acc[3 * h + j, dst, :] = r[:, 128 * j:128 * j + 128]

    def some(h, g, blocks, fresh):
        src, dst = rows_of(g)
        r = None
        for kind, steps in blocks:
            block = (xh if kind == "o" else 1 - xh) * 8 + (z + steps) % 8
            at = pl.ds(pl.multiple_of(block * 256, 256), 256)
            d = jnp.dot(tok[src, at], wts[h, at, :], preferred_element_type=jnp.float32)
            r = d if r is None else r + d
        for j in range(3):
            part = r[:, 128 * j:128 * j + 128]
            acc[3 * h + j, dst, :] = part if fresh else acc[3 * h + j, dst, :] + part

    def over(order, work):
        count, place_of = order
        def one(i, _):
            work(seg(*place_of(i)))
            return 0
        lax.fori_loop(0, count, one, 0)

    near = (4, lambda i: (i // 3, i % 3 + (i % 3) // 2))
    near_a = (2, lambda i: (0, i))
    near_b = (2, lambda i: (i, 3 - 3 * i))
    side = (2, lambda i: (1, 1 + 2 * i))
    far_a = (1, lambda i: (0, 2))
    far_b = (1, lambda i: (1, 2))
    seven = (7, lambda i: ((i + 1) // 4 - (i + 1) // 8, (i + 1) % 4 - (i // 6) * 3))
    every = (8, lambda i: (i // 4, i % 4))
    groups = [
        [("o", 0), ("p", 0), ("o", 7), ("o", 1)],
        [("o", 6), ("p", 1), ("p", 7), ("p", 2)],
        [("o", 5), ("o", 2), ("p", 6), ("p", 3)],
        [("o", 4), ("o", 3), ("p", 5), ("p", 4)],
    ]
    firsts = (6, lambda i: (i // 3, i % 3 + (i % 3) // 2))
    ways = {("o", 7): (0, 1), ("o", 6): (0, 2), ("o", 5): (0, 3), ("o", 4): (0, 4), ("p", 7): (0, 1), ("p", 6): (0, 2), ("p", 5): (0, 3),
            ("o", 1): (1, 1), ("o", 2): (1, 2), ("o", 3): (1, 3), ("p", 1): (1, 1), ("p", 2): (1, 2), ("p", 3): (1, 3), ("p", 4): (1, 4),
            ("p", 0): (0, 0)}

    def have(h, blocks):
        for kind, steps in blocks:
            if (kind, steps) != ("o", 0):
                way, far = ways[kind, steps]
                w_arrive(way, kind, far, h)

    z_step(2)
    z_step(3)
    z_step(4)
    z_step(5)
    arrive("BU", "BD")
    push("B", 0, 1, None, across, "BXU")
    push("B", 0, 3, 0, up, "BO0")
    push("B", 0, 1, 1, down, "BO1")
    push("B", 0, 3, None, across, "BXD")
    arrive("AX")
    push("A", 1, 0, None, up, "AXD")
    push("A", 1, 0, None, down, "AXU")
    arrive("AU", "AD")
    push("A", 0, 3, 0, up, "AO0")
    push("A", 0, 1, 1, down, "AO1")
    arrive("BX")
    z_step(6)
    remote(own, own, d_send.at[len(NAMES)], d_recv.at[len(NAMES)], sib).wait_recv()
    other("BU", "BD", "AX", "AU", "AD", "BX")
    have(1, groups[0])
    over(near, lambda g: some(1, g, groups[0], True))
    arrive("BO0", "BO1")
    push("B", 0, 2, 0, across, "BXO0")
    push("B", 0, 2, 1, across, "BXO1")
    z_step(7)
    z_step(8)
    z_step(9)
    have(0, [key for group in groups for key in group])
    over(near_a, lambda g: whole(0, g))
    arrive("AXU", "AXD")
    push("A", 1, 3, 0, up, "AXO0")
    push("A", 1, 1, 1, down, "AXO1")
    z_step(10)
    over(near_b, lambda g: whole(0, g))
    arrive("BXU", "BXD")
    other("AXU", "AXD", "BXU", "BXD")
    over(side, lambda g: whole(0, g))
    z_step(11)
    have(1, groups[1])
    over(side, lambda g: some(1, g, groups[0] + groups[1], True))
    over(near, lambda g: some(1, g, groups[1], False))
    arrive("AO0", "AO1")
    other("BO0", "BO1", "AO0", "AO1")
    over(far_a, lambda g: whole(0, g))
    z_step(12)
    z_step(13)
    have(1, groups[2])
    over(far_a, lambda g: some(1, g, groups[0] + groups[1] + groups[2], True))
    over(firsts, lambda g: some(1, g, groups[2], False))
    arrive("BXO0", "BXO1", "AXO0", "AXO1")
    other("BXO0", "BXO1", "AXO0", "AXO1")
    over(far_b, lambda g: whole(0, g))
    over(far_b, lambda g: some(1, g, groups[0] + groups[1] + groups[2], True))

    def channels(h):
        return pl.ds(pl.multiple_of(s * 256 + h * 128, 128), 128)

    def block_copy(h, n, core):
        dx, dy = nth(n)
        block = pl.ds(pl.multiple_of((seg(dx, dy) * 2 + core) * 128, 128), 128)
        return remote(stage.at[h, block, :], out.at[0, :, channels(h)], o_send.at[h, n, core], o_recv.at[h, n, c], dev(dx, dy, core))

    def to_sibling(h):
        block = own_rows(1 - c)
        return remote(stage.at[h, block, :], out.at[0, :, channels(h)], o_send.at[h, 0, 0], o_recv.at[h, 0, 0], sib)

    def to_self(h):
        return pltpu.make_async_copy(stage.at[h, own_rows(c), :], out.at[0, :, channels(h)], o_local.at[h])

    def emit(h, core):
        def cast(g, _):
            src = pl.ds(pl.multiple_of(g * PITCH + core * 128, 8), 128)
            dst = pl.ds(pl.multiple_of(g * SPAN + core * 128, 128), 128)
            stage[h, dst, :] = res[src, :].astype(jnp.bfloat16)
            return 0
        lax.fori_loop(0, SEGS, cast, 0)
        def go(n, _):
            block_copy(h, n, core).start()
            return 0
        lax.fori_loop(1, 8, go, 0)
        if core:
            to_sibling(h).start()
            to_self(h).start()

    for h in HALVES:
        if h:
            have(1, groups[3])
            over(every, lambda g: some(1, g, groups[3], False))
        lanes = slice(h * 128, h * 128 + 128)
        conv_half(h, acc, prod, res, taps, rates[:, lanes], gains[:, lanes], skip[:, lanes], functools.partial(emit, h))

    for h in HALVES:
        def finish(n, _):
            for core in range(2):
                block_copy(h, n, core).wait_send()
                ref = out.at[0, :, channels(h)]
                remote(ref, ref, o_send.at[h, n, core], o_recv.at[h, n, core], sib).wait_recv()
            return 0
        lax.fori_loop(1, 8, finish, 0)
        to_sibling(h).wait()
        to_self(h).wait()
    for copy in sends:
        copy.wait_send()


def body(tokens, w_query, w_key, w_value, short_taps, residue, decay, passthrough):
    vmem, anywhere = pl.BlockSpec(memory_space=pltpu.VMEM), pl.BlockSpec(memory_space=pl.ANY)
    dma = pltpu.SemaphoreType.DMA
    return pl.pallas_call(
        kernel,
        out_shape=jax.ShapeDtypeStruct((1, 128, 4096), jnp.bfloat16),
        in_specs=[anywhere] * 4 + [vmem] * 4,
        out_specs=vmem,
        scratch_shapes=[
            pltpu.VMEM((2048, 4096), jnp.bfloat16),
            pltpu.VMEM((2, 4096, 384), jnp.bfloat16),
            pltpu.VMEM((3, 256, 256), jnp.float32),
            pltpu.VMEM((6, SEGS * PITCH, 128), jnp.float32),
            pltpu.VMEM((2048, 128), jnp.float32),
            pltpu.VMEM((SEGS * PITCH, 128), jnp.float32),
            pltpu.VMEM((2, 2048, 128), jnp.bfloat16),
            dma((4,)),
            dma((2, 14)), dma((2, 14)),
            dma((2,)), dma((2,)),
            dma((len(NAMES),)), dma((len(NAMES),)),
            dma((len(NAMES) + 1,)), dma((len(NAMES) + 1,)),
            dma((2, 8, 2)), dma((2, 8, 2)), dma((2,)),
        ],
        compiler_params=pltpu.CompilerParams(collective_id=0, has_side_effects=True, vmem_limit_bytes=50 << 20),
        cost_estimate=pl.CostEstimate(flops=2 * 2048 * 4096 * 768, bytes_accessed=4 << 20, transcendentals=0),
    )(tokens, w_query, w_key, w_value, short_taps, residue, decay, passthrough[None])


def solution(mesh):
    return jax.shard_map(
        body,
        mesh=mesh,
        in_specs=(
            P("fsdp", "seq", None),
            P("fsdp", "seq"),
            P("fsdp", "seq"),
            P("fsdp", "seq"),
            P(None, None, "seq"),
            P("seq", None),
            P("seq", None),
            P("seq"),
        ),
        out_specs=P("fsdp", "seq", None),
        check_vma=False,
    )
```

time: 282 us -> 112 us (0.40)
  waiting for transfers between devices: 213 us -> 0 us
  Pallas kernels: 11.2 us -> 106 us
  blocking collectives: 20.2 us -> 0 us
  matrix products: 18.2 us -> 0 us
  between operations: 13.5 us -> 0.05 us
  local copies, waits for them, and re-layouts: 2.77 us -> 5.79 us
  other arithmetic: 2.9 us -> 0 us
    all_gather x2 -> x0, waiting for transfers between devices: 212 us -> none  [the longest x1 118 us: body(): weights = lax.all_gather(masters, 'fsdp', axis=0, tiled=True)]
    pallas_call x1, Pallas kernels: 11.2 us -> 106 us  [body(): pl.pallas_call(kernel, out_shape=jax.ShapeDtypeStruct((1, 128, 4096), jnp...]
    all_to_all x1 -> x0, blocking collectives: 20.2 us -> none  [body(): lax.all_to_all(result, 'seq', split_axis=0, concat_axis=1, tiled=True)[None]]
    dot_general x1 -> x0, matrix products: 18.2 us -> none  [body(): projected = jnp.dot(inputs, weights, preferred_element_type=jnp.float32)]
    unnamed x15, local copies, waits for them, and re-layouts: 0.86 us -> 5.79 us
    convert_element_type x3 -> x0, other arithmetic: 2.9 us -> none  [body(): masters = [w.astype(jnp.bfloat16) for w in (w_query, w_key, w_value)]]
  transfers between devices with their start and end apart: 2 -> 0, of which waited for: 2 -> 0; matrix products, arithmetic and copies ran while one was open for 0% -> 0% of each run, Pallas kernels for 0% -> 0%
where the time goes in v2:
time: 112 us
  Pallas kernels  106 us (95%)
  local copies, waits for them, and re-layouts  5.79 us (5%)
    pallas_call x1, Pallas kernels, body(): pl.pallas_call(kernel, out_shape=jax.ShapeDtypeStruct((1, 128, 4096), jnp...  106 us
    unnamed x15, local copies, waits for them, and re-layouts  5.79 us

profile of v2, /device:TPU:1, one launch (start us, length us, event | category | flops | bytes accessed | tf_op | source)
XLA Modules:
  0.0 111.9 jit_solution(1245935088611577443)
XLA Ops:
  0.0 0.0 copy-start.1
  0.0 0.9 copy.9.residue
  0.9 0.0 copy-start.4
  0.9 0.0 copy-start.5
  0.9 0.8 copy.10.decay
  1.7 0.0 copy-done.1
  1.7 0.0 copy-done.4
  1.7 0.0 copy-done.5
  1.7 0.0 copy-start
  1.7 1.2 %copy-done = bf16[1,128,4096]{2,1,0:T(8,128)(2,1)S(1)} copy-done((bf16[1,128,4096]{2,1,0:T(8,128)(2,1)S(1)}, bf16[1,128,4096]{2,1,0:T(8,128)(2,1)}, u32[]{:S(2)}) %copy-start) | copy-done | bytes 1048600
  3.0 0.0 copy-start.2
  3.0 0.9 copy-done.2
  3.9 0.0 copy-start.3
  3.9 0.9 copy-done.3
  4.9 106.0 %shard_map.82 = bf16[1,128,4096]{2,1,0:T(8,128)(2,1)S(1)} custom-call(bf16[1,128,4096]{2,1,0:T(8,128)(2,1)S(1)} %copy-done, f32[256,256]{1,0:T(8,128)S(1)} %copy-done.1, f32[256,256]{1,0:T(8,128)S(1)} %copy-done.2, f32[256,256]{1,0:T(8,128)S(1)} %copy-done.3, f32[3,3,256]{2,1,0:T(4,128)S(1)} %copy-done.4, f32[256,16]{1,0:T(8,128)S(1)} %copy.9.residue, ...), custom_call_target="tpu_custom_call" | custom-call | flops 12884901888 | bytes 4194304 | tf_op jit(solution)/shard_map/pallas_call | solution.py:377
  110.9 1.0 copy.12
Async XLA Ops:
  0.0 1.7 %copy-start.1 = (f32[256,256]{1,0:T(8,128)S(1)}, f32[256,256]{1,0:T(8,128)}, u32[]{:S(2)}) copy-start(f32[256,256]{1,0:T(8,128)} %w_query.1) | copy-start | bytes 786436
  0.9 0.9 copy-start.4
  0.9 0.9 copy-start.5
  1.7 1.2 %copy-start = (bf16[1,128,4096]{2,1,0:T(8,128)(2,1)S(1)}, bf16[1,128,4096]{2,1,0:T(8,128)(2,1)}, u32[]{:S(2)}) copy-start(bf16[1,128,4096]{2,1,0:T(8,128)(2,1)} %tokens.1) | copy-start | bytes 3145732
  3.0 0.9 copy-start.2
  3.9 0.9 copy-start.3

commit v3 on v2

--- a/solution.py
+++ b/solution.py
@@ -11,13 +11,13 @@
 MODES = 16
 SEGS, SPAN = 8, 256
 PITCH = 264
-SPLIT = 9 * 256
+SPLIT = 10 * 256
 HALVES = (0, 1)
 
-UP = [("o", 0, 0), ("o", 0, 1), ("o", 1, 0), ("p", 0, 0), ("o", 2, 0), ("p", 1, 0), ("o", 3, 0), ("p", 2, 0),
-      ("o", 1, 1), ("p", 0, 1), ("o", 2, 1), ("p", 1, 1), ("o", 3, 1), ("p", 2, 1)]
-DOWN = [("o", 0, 0), ("o", 0, 1), ("p", 0, 0), ("o", 1, 0), ("p", 1, 0), ("o", 2, 0), ("p", 2, 0), ("p", 0, 1),
-        ("p", 3, 0), ("p", 1, 1), ("o", 1, 1), ("p", 2, 1), ("o", 2, 1), ("p", 3, 1)]
+UP = [("o", 0, 0), ("o", 0, 1), ("p", 0, 0), ("p", 0, 1), ("o", 1, 0), ("o", 1, 1), ("p", 1, 0), ("p", 1, 1),
+      ("o", 2, 0), ("p", 2, 0), ("o", 2, 1), ("o", 3, 0), ("p", 2, 1), ("o", 3, 1)]
+DOWN = [("o", 0, 0), ("o", 0, 1), ("p", 0, 0), ("p", 0, 1), ("o", 1, 0), ("p", 1, 0), ("o", 1, 1), ("p", 1, 1),
+        ("p", 2, 0), ("o", 2, 0), ("p", 2, 1), ("p", 3, 0), ("o", 2, 1), ("p", 3, 1)]
 
 PIECES = {
     "AX": ("A", 1, 0, None), "AU": ("A", 0, 1, None), "AD": ("A", 0, 3, None), "AXU": ("A", 1, 1, None), "AXD": ("A", 1, 3, None),
@@ -80,8 +80,8 @@
         emit(core)
 
 
-def kernel(tokens, w_query, w_key, w_value, taps, residue, decay, skip, out,
-           tok, wts, masters, acc, prod, res, stage,
+def kernel(tokens, w_query, w_key, w_value, taps_in, residue_in, decay_in, skip_in, out,
+           taps, residue, decay, skip, tok, wts, masters, acc, prod, res, stage,
            load_sem, z_send, z_recv, h_send, h_recv, t_send, t_recv, d_send, d_recv, o_send, o_recv, o_local):
     s, f = lax.axis_index("seq"), lax.axis_index("fsdp")
     xl, y, c = s // 8, (s // 2) % 4, s % 2
@@ -118,6 +118,8 @@
 
     loads = [pltpu.make_async_copy(w, masters.at[j], load_sem.at[j]) for j, w in enumerate((w_query, w_key, w_value))]
     loads.append(pltpu.make_async_copy(tokens.at[0], tok.at[own_rows(c), :], load_sem.at[3]))
+    small = ((taps_in, taps), (residue_in, residue), (decay_in, decay), (skip_in, skip))
+    loads += [pltpu.make_async_copy(src, dst, load_sem.at[4 + i]) for i, (src, dst) in enumerate(small)]
     for load in loads:
         load.start()
     for load in loads[:3]:
@@ -126,9 +128,6 @@
     for h in HALVES:
         for j in range(3):
             wts[h, mine, 128 * j:128 * j + 128] = masters[j, :, 128 * h:128 * h + 128].astype(jnp.bfloat16)
-    rates = decay[...].T
-    gains = residue[...].T * jnp.sqrt(rates)
-    loads[3].wait()
     pl.semaphore_wait(barrier, 18)
 
     def t_ref(part, dx, dy, rows, core):
@@ -166,9 +165,6 @@
             shared.add(name)
 
     up, down, across = dev(0, 1, c), dev(0, 3, c), dev(1, 0, c)
-    push("A", 0, 0, None, across, "AX")
-    push("B", 0, 0, None, up, "BD")
-    push("B", 0, 0, None, down, "BU")
 
     def w_ref(h, kind, steps):
         block = (xh if kind == "o" else 1 - xh) * 8 + (z + steps) % 8
@@ -203,13 +199,17 @@
             copy.start()
             sends.append(copy)
 
-    hop[0].start()
+    for copy in hop:
+        copy.start()
     z_step(0)
+    loads[3].wait()
+    push("B", 0, 0, None, up, "BD")
+    push("B", 0, 0, None, down, "BU")
+    push("A", 0, 0, None, across, "AX")
+    z_step(1)
     push("A", 0, 0, None, up, "AD")
     push("A", 0, 0, None, down, "AU")
     push("B", 0, 0, None, across, "BX")
-    z_step(1)
-    hop[1].start()
     own = tok.at[own_rows(c), :]
     share(len(NAMES), own)
 
@@ -241,21 +241,21 @@
             return 0
         lax.fori_loop(0, count, one, 0)
 
-    near = (4, lambda i: (i // 3, i % 3 + (i % 3) // 2))
-    near_a = (2, lambda i: (0, i))
-    near_b = (2, lambda i: (i, 3 - 3 * i))
-    side = (2, lambda i: (1, 1 + 2 * i))
-    far_a = (1, lambda i: (0, 2))
-    far_b = (1, lambda i: (1, 2))
-    seven = (7, lambda i: ((i + 1) // 4 - (i + 1) // 8, (i + 1) % 4 - (i // 6) * 3))
+    near = (3, lambda i: (0, i + i // 2))
+    beside = (1, lambda i: (1, 0))
+    side_up = (1, lambda i: (1, 1))
+    side_down = (1, lambda i: (1, 3))
+    opposite = (1, lambda i: (0, 2))
+    last = (1, lambda i: (1, 2))
     every = (8, lambda i: (i // 4, i % 4))
     groups = [
-        [("o", 0), ("p", 0), ("o", 7), ("o", 1)],
-        [("o", 6), ("p", 1), ("p", 7), ("p", 2)],
-        [("o", 5), ("o", 2), ("p", 6), ("p", 3)],
-        [("o", 4), ("o", 3), ("p", 5), ("p", 4)],
+        [("o", 0), ("p", 0), ("o", 7), ("o", 1), ("p", 7), ("p", 1)],
+        [("o", 6), ("o", 2), ("p", 6), ("p", 2)],
+        [("o", 5), ("o", 3), ("p", 5), ("p", 3)],
+        [("o", 4), ("p", 4)],
     ]
-    firsts = (6, lambda i: (i // 3, i % 3 + (i % 3) // 2))
+    late = [("o", 3), ("p", 5), ("o", 4), ("p", 4)]
+    firsts = (4, lambda i: (i // 3, i % 3 + (i % 3) // 2))
     ways = {("o", 7): (0, 1), ("o", 6): (0, 2), ("o", 5): (0, 3), ("o", 4): (0, 4), ("p", 7): (0, 1), ("p", 6): (0, 2), ("p", 5): (0, 3),
             ("o", 1): (1, 1), ("o", 2): (1, 2), ("o", 3): (1, 3), ("p", 1): (1, 1), ("p", 2): (1, 2), ("p", 3): (1, 3), ("p", 4): (1, 4),
             ("p", 0): (0, 0)}
@@ -267,58 +267,70 @@
                 w_arrive(way, kind, far, h)
 
     z_step(2)
+    arrive("BU", "BD")
+    push("B", 0, 3, 0, up, "BO0")
+    push("B", 0, 1, 1, down, "BO1")
+    push("B", 0, 1, None, across, "BXU")
+    push("B", 0, 3, None, across, "BXD")
     z_step(3)
     z_step(4)
     z_step(5)
-    arrive("BU", "BD")
-    push("B", 0, 1, None, across, "BXU")
-    push("B", 0, 3, 0, up, "BO0")
-    push("B", 0, 1, 1, down, "BO1")
-    push("B", 0, 3, None, across, "BXD")
+    z_step(6)
+    z_step(7)
     arrive("AX")
     push("A", 1, 0, None, up, "AXD")
     push("A", 1, 0, None, down, "AXU")
     arrive("AU", "AD")
     push("A", 0, 3, 0, up, "AO0")
     push("A", 0, 1, 1, down, "AO1")
-    arrive("BX")
-    z_step(6)
+    z_step(8)
     remote(own, own, d_send.at[len(NAMES)], d_recv.at[len(NAMES)], sib).wait_recv()
-    other("BU", "BD", "AX", "AU", "AD", "BX")
+    other("BU", "BD", "AU", "AD", "AX")
+    have(0, groups[0])
     have(1, groups[0])
-    over(near, lambda g: some(1, g, groups[0], True))
+    over(near, lambda g: some(0, g, groups[0], True))
     arrive("BO0", "BO1")
     push("B", 0, 2, 0, across, "BXO0")
     push("B", 0, 2, 1, across, "BXO1")
-    z_step(7)
-    z_step(8)
+    over(near, lambda g: some(1, g, groups[0], True))
     z_step(9)
-    have(0, [key for group in groups for key in group])
-    over(near_a, lambda g: whole(0, g))
-    arrive("AXU", "AXD")
+    arrive("BX")
+    other("BX", "BO0", "BO1")
+    over(beside, lambda g: some(0, g, groups[0], True))
+    over(beside, lambda g: some(1, g, groups[0], True))
+    z_step(10)
+    have(0, groups[1])
+    have(1, groups[1])
+    over(firsts, lambda g: some(0, g, groups[1], False))
+    z_step(11)
+    over(firsts, lambda g: some(1, g, groups[1], False))
+    arrive("BXU", "AXU", "AXD")
     push("A", 1, 3, 0, up, "AXO0")
     push("A", 1, 1, 1, down, "AXO1")
-    z_step(10)
-    over(near_b, lambda g: whole(0, g))
-    arrive("BXU", "BXD")
-    other("AXU", "AXD", "BXU", "BXD")
-    over(side, lambda g: whole(0, g))
-    z_step(11)
-    have(1, groups[1])
-    over(side, lambda g: some(1, g, groups[0] + groups[1], True))
-    over(near, lambda g: some(1, g, groups[1], False))
-    arrive("AO0", "AO1")
-    other("BO0", "BO1", "AO0", "AO1")
-    over(far_a, lambda g: whole(0, g))
     z_step(12)
+    other("BXU", "AXU", "AXD")
+    have(0, groups[2])
+    first_ten = groups[0] + groups[1]
+    over(side_up, lambda g: some(0, g, first_ten + groups[2], True))
+    over(side_up, lambda g: some(1, g, first_ten, True))
+    over(firsts, lambda g: some(0, g, groups[2], False))
     z_step(13)
-    have(1, groups[2])
-    over(far_a, lambda g: some(1, g, groups[0] + groups[1] + groups[2], True))
-    over(firsts, lambda g: some(1, g, groups[2], False))
+    arrive("AO0", "AO1", "BXD")
+    other("AO0", "AO1", "BXD")
+    early = [("o", 5), ("p", 3)]
+    have(1, early)
+    over(firsts, lambda g: some(1, g, early, False))
+    over(side_up, lambda g: some(1, g, early, False))
+    have(0, groups[3])
+    over(side_down, lambda g: whole(0, g))
+    over(opposite, lambda g: whole(0, g))
+    over(firsts, lambda g: some(0, g, groups[3], False))
+    over(side_up, lambda g: some(0, g, groups[3], False))
     arrive("BXO0", "BXO1", "AXO0", "AXO1")
+    over(side_down, lambda g: some(1, g, first_ten + early, True))
+    over(opposite, lambda g: some(1, g, first_ten + early, True))
     other("BXO0", "BXO1", "AXO0", "AXO1")
-    over(far_b, lambda g: whole(0, g))
-    over(far_b, lambda g: some(1, g, groups[0] + groups[1] + groups[2], True))
+    over(last, lambda g: whole(0, g))
 
     def channels(h):
         return pl.ds(pl.multiple_of(s * 256 + h * 128, 128), 128)
@@ -334,6 +346,11 @@
 
     def to_self(h):
         return pltpu.make_async_copy(stage.at[h, own_rows(c), :], out.at[0, :, channels(h)], o_local.at[h])
+
+    for load in loads[4:]:
+        load.wait()
+    rates = decay[...]
+    gains = residue[...] * jnp.sqrt(rates)
 
     def emit(h, core):
         def cast(g, _):
@@ -352,10 +369,11 @@
 
     for h in HALVES:
         if h:
-            have(1, groups[3])
-            over(every, lambda g: some(1, g, groups[3], False))
+            over(last, lambda g: some(1, g, first_ten + early, True))
+            have(1, late)
+            over(every, lambda g: some(1, g, late, False))
         lanes = slice(h * 128, h * 128 + 128)
-        conv_half(h, acc, prod, res, taps, rates[:, lanes], gains[:, lanes], skip[:, lanes], functools.partial(emit, h))
+        conv_half(h, acc, prod, res, taps, rates[:, lanes], gains[:, lanes], skip[0:1, lanes], functools.partial(emit, h))
 
     for h in HALVES:
         def finish(n, _):
@@ -372,14 +390,18 @@
 
 
 def body(tokens, w_query, w_key, w_value, short_taps, residue, decay, passthrough):
-    vmem, anywhere = pl.BlockSpec(memory_space=pltpu.VMEM), pl.BlockSpec(memory_space=pl.ANY)
+    hbm = pl.BlockSpec(memory_space=pltpu.HBM)
     dma = pltpu.SemaphoreType.DMA
     return pl.pallas_call(
         kernel,
         out_shape=jax.ShapeDtypeStruct((1, 128, 4096), jnp.bfloat16),
-        in_specs=[anywhere] * 4 + [vmem] * 4,
-        out_specs=vmem,
+        in_specs=[hbm] * 8,
+        out_specs=hbm,
         scratch_shapes=[
+            pltpu.VMEM((3, 3, 256), jnp.float32),
+            pltpu.VMEM((MODES, 256), jnp.float32),
+            pltpu.VMEM((MODES, 256), jnp.float32),
+            pltpu.VMEM((1, 256), jnp.float32),
             pltpu.VMEM((2048, 4096), jnp.bfloat16),
             pltpu.VMEM((2, 4096, 384), jnp.bfloat16),
             pltpu.VMEM((3, 256, 256), jnp.float32),
@@ -387,16 +409,16 @@
             pltpu.VMEM((2048, 128), jnp.float32),
             pltpu.VMEM((SEGS * PITCH, 128), jnp.float32),
             pltpu.VMEM((2, 2048, 128), jnp.bfloat16),
-            dma((4,)),
+            dma((8,)),
             dma((2, 14)), dma((2, 14)),
             dma((2,)), dma((2,)),
             dma((len(NAMES),)), dma((len(NAMES),)),
             dma((len(NAMES) + 1,)), dma((len(NAMES) + 1,)),
             dma((2, 8, 2)), dma((2, 8, 2)), dma((2,)),
         ],
-        compiler_params=pltpu.CompilerParams(collective_id=0, has_side_effects=True, vmem_limit_bytes=50 << 20),
+        compiler_params=pltpu.CompilerParams(collective_id=0, has_side_effects=True, vmem_limit_bytes=(64 << 20) - (1 << 16)),
         cost_estimate=pl.CostEstimate(flops=2 * 2048 * 4096 * 768, bytes_accessed=4 << 20, transcendentals=0),
-    )(tokens, w_query, w_key, w_value, short_taps, residue, decay, passthrough[None])
+    )(tokens, w_query, w_key, w_value, short_taps, residue.T, decay.T, passthrough[None])
 
 
 def solution(mesh):

time: 112 us -> 97.5 us (0.87)
  Pallas kernels: 106 us -> 95 us
  local copies, waits for them, and re-layouts: 5.79 us -> 2.29 us
    pallas_call x1, Pallas kernels: 106 us -> 95 us  [body(): pl.pallas_call(kernel, out_shape=jax.ShapeDtypeStruct((1, 128, 4096), jnp...]
    unnamed x15 -> x1, local copies, waits for them, and re-layouts: 5.79 us -> 2.29 us
where the time goes in v3:
time: 97.5 us; the launch traced here: 97.3 us
  Pallas kernels  95 us (97%)
  local copies, waits for them, and re-layouts  2.29 us (2%)
    pallas_call x1, Pallas kernels, body(): pl.pallas_call(kernel, out_shape=jax.ShapeDtypeStruct((1, 128, 4096), jnp...  95 us
    unnamed x1, local copies, waits for them, and re-layouts  2.29 us

profile of v3, /device:TPU:1, one launch (start us, length us, event | category | flops | bytes accessed | tf_op | source)
XLA Modules:
  0.0 97.3 jit_solution(12875962737971526747)
XLA Ops:
  0.0 95.0 %shard_map.82 = bf16[1,128,4096]{2,1,0:T(8,128)(2,1)} custom-call(bf16[1,128,4096]{2,1,0:T(8,128)(2,1)} %tokens.1, f32[256,256]{1,0:T(8,128)} %w_query.1, f32[256,256]{1,0:T(8,128)} %w_key.1, f32[256,256]{1,0:T(8,128)} %w_value.1, f32[3,3,256]{2,1,0:T(4,128)} %taps_in.1, f32[16,256]{1,0:T(8,128)} %bitcast.3, f32[16,256]{1,0:T(8,128)} %bitcast.4, ...), custom_call_target="tpu_custom_call" | custom-call | flops 12884901888 | bytes 4194304 | tf_op jit(solution)/shard_map/pallas_call | solution.py:395
  95.1 2.3 %copy.10 = bf16[1,128,4096]{2,1,0:T(8,128)(2,1)} copy(bf16[1,128,4096]{2,1,0:T(8,128)(2,1)} %shard_map.82) | data formatting | bytes 2097152

commit v4 on v3

--- a/solution.py
+++ b/solution.py
@@ -32,7 +32,7 @@
     return jnp.where(row >= n, pltpu.roll(v, n, 0), 0.0)
 
 
-def conv_half(half, acc, prod, res, taps, rates, gains, skip, emit):
+def conv_half(half, acc, prod, res, taps, rates, gains, skip, emit, ready=None, beside=None):
     row = lax.broadcasted_iota(jnp.int32, (SEGS, 128), 0)
     wide = lambda v: jnp.broadcast_to(v, (SEGS, 128))
     fade = [wide(jnp.exp(-rates[r:r + 1])) for r in range(MODES)]
@@ -74,9 +74,20 @@
         res[pl.ds(t, SEGS, stride=PITCH), :] = (tap[0][0] * q + tap[0][1] * q1 + tap[0][2] * q2) * parts[0]
         return q, q1, hs
 
+    def stretch(i, carry):
+        beside(i)
+        for u in range(SPAN // 8):
+            carry = second(i * (SPAN // 8) + u, carry)
+        return carry
+
+    if ready:
+        ready()
     carry = (*before(0), tuple(start))
     for core in range(2):
-        carry = lax.fori_loop(core * (SPAN // 2), (core + 1) * (SPAN // 2), second, carry, unroll=8)
+        if beside:
+            carry = lax.fori_loop(4 * core, 4 * core + 4, stretch, carry)
+        else:
+            carry = lax.fori_loop(core * (SPAN // 2), (core + 1) * (SPAN // 2), second, carry, unroll=8)
         emit(core)
 
 
@@ -87,7 +98,12 @@
     xl, y, c = s // 8, (s // 2) % 4, s % 2
     xh, z = f // 8, f % 8
 
+    planes, rings = [xl * 4, (1 - xl) * 4], [y] + [(y + dy) % 4 for dy in (1, 2, 3)]
+    chips = [[plane + ring for ring in rings] for plane in planes]
+
     def seg(dx, dy):
+        if isinstance(dx, int) and isinstance(dy, int):
+            return chips[dx % 2][dy % 4]
         return ((xl + dx) % 2) * 4 + (y + dy) % 4
 
     def dev(dx, dy, core):
@@ -103,12 +119,9 @@
 
     barrier = pltpu.get_barrier_semaphore()
 
-    def greet(n, _):
+    for n in range(1, 8):
         for core in range(2):
             pl.semaphore_signal(barrier, inc=1, device_id=dev(*nth(n), core), device_id_type=MESH)
-        return 0
-
-    lax.fori_loop(1, 8, greet, 0)
     for d in (*z_dev, h_dev, sib):
         pl.semaphore_signal(barrier, inc=1, device_id=d, device_id_type=MESH)
 
@@ -166,9 +179,11 @@
 
     up, down, across = dev(0, 1, c), dev(0, 3, c), dev(1, 0, c)
 
+    around = [z] + [(z + steps) % 8 for steps in range(1, 8)]
+    starts = {(kind, steps): (half * 8 + around[steps]) * 256 for kind, half in (("o", xh), ("p", 1 - xh)) for steps in range(8)}
+
     def w_ref(h, kind, steps):
-        block = (xh if kind == "o" else 1 - xh) * 8 + (z + steps) % 8
-        return wts.at[h, pl.ds(pl.multiple_of(block * 256, 256), 256), :]
+        return wts.at[h, pl.ds(pl.multiple_of(starts[kind, steps % 8], 256), 256), :]
 
     hop = [remote(w_ref(h, "o", 0), w_ref(h, "o", 0), h_send.at[h], h_recv.at[h], h_dev) for h in HALVES]
     sends.extend(hop)
@@ -226,13 +241,16 @@
         src, dst = rows_of(g)
         r = None
         for kind, steps in blocks:
-            block = (xh if kind == "o" else 1 - xh) * 8 + (z + steps) % 8
-            at = pl.ds(pl.multiple_of(block * 256, 256), 256)
+            at = pl.ds(pl.multiple_of(starts[kind, steps], 256), 256)
             d = jnp.dot(tok[src, at], wts[h, at, :], preferred_element_type=jnp.float32)
             r = d if r is None else r + d
         for j in range(3):
             part = r[:, 128 * j:128 * j + 128]
             acc[3 * h + j, dst, :] = part if fresh else acc[3 * h + j, dst, :] + part
+
+    def empty(g):
+        for j in range(3):
+            acc[3 + j, rows_of(g)[1], :] = jnp.zeros((SPAN, 128), jnp.float32)
 
     def over(order, work):
         count, place_of = order
@@ -326,6 +344,7 @@
     over(opposite, lambda g: whole(0, g))
     over(firsts, lambda g: some(0, g, groups[3], False))
     over(side_up, lambda g: some(0, g, groups[3], False))
+    over(last, empty)
     arrive("BXO0", "BXO1", "AXO0", "AXO1")
     over(side_down, lambda g: some(1, g, first_ten + early, True))
     over(opposite, lambda g: some(1, g, first_ten + early, True))
@@ -354,35 +373,30 @@
 
     def emit(h, core):
         def cast(g, _):
-            src = pl.ds(pl.multiple_of(g * PITCH + core * 128, 8), 128)
-            dst = pl.ds(pl.multiple_of(g * SPAN + core * 128, 128), 128)
+            src, dst = pl.ds(g * PITCH + core * 128, 128), pl.ds(g * SPAN + core * 128, 128)
             stage[h, dst, :] = res[src, :].astype(jnp.bfloat16)
             return 0
-        lax.fori_loop(0, SEGS, cast, 0)
-        def go(n, _):
+        for g in range(SEGS):
+            cast(g, 0)
+        for n in range(1, 8):
             block_copy(h, n, core).start()
-            return 0
-        lax.fori_loop(1, 8, go, 0)
         if core:
             to_sibling(h).start()
             to_self(h).start()
 
     for h in HALVES:
         if h:
-            over(last, lambda g: some(1, g, first_ten + early, True))
-            have(1, late)
-            over(every, lambda g: some(1, g, late, False))
+            over(last, lambda g: some(1, g, first_ten + early, False))
         lanes = slice(h * 128, h * 128 + 128)
-        conv_half(h, acc, prod, res, taps, rates[:, lanes], gains[:, lanes], skip[0:1, lanes], functools.partial(emit, h))
+        conv_half(h, acc, prod, res, taps, rates[:, lanes], gains[:, lanes], skip[0:1, lanes], functools.partial(emit, h),
+                  *(() if h else (lambda: have(1, late), lambda g: some(1, g, late, False))))
 
     for h in HALVES:
-        def finish(n, _):
+        for n in range(1, 8):
             for core in range(2):
                 block_copy(h, n, core).wait_send()
                 ref = out.at[0, :, channels(h)]
                 remote(ref, ref, o_send.at[h, n, core], o_recv.at[h, n, core], sib).wait_recv()
-            return 0
-        lax.fori_loop(1, 8, finish, 0)
         to_sibling(h).wait()
         to_self(h).wait()
     for copy in sends:

time: 97.5 us -> 96.4 us (0.989)
  Pallas kernels: 95 us -> 94 us
    pallas_call x1, Pallas kernels: 95 us -> 94 us  [body(): pl.pallas_call(kernel, out_shape=jax.ShapeDtypeStruct((1, 128, 4096), jnp...]
where the time goes in v4:
time: 96.4 us; the launch traced here: 96.3 us
  Pallas kernels  94 us (98%)
  local copies, waits for them, and re-layouts  2.29 us (2%)
    pallas_call x1, Pallas kernels, body(): pl.pallas_call(kernel, out_shape=jax.ShapeDtypeStruct((1, 128, 4096), jnp...  94 us
    unnamed x1, local copies, waits for them, and re-layouts  2.29 us

profile of v4, /device:TPU:1, one launch (start us, length us, event | category | flops | bytes accessed | tf_op | source)
XLA Modules:
  0.0 96.3 jit_solution(7658945832450531369)
XLA Ops:
  0.0 94.0 %shard_map.82 = bf16[1,128,4096]{2,1,0:T(8,128)(2,1)} custom-call(bf16[1,128,4096]{2,1,0:T(8,128)(2,1)} %tokens.1, f32[256,256]{1,0:T(8,128)} %w_query.1, f32[256,256]{1,0:T(8,128)} %w_key.1, f32[256,256]{1,0:T(8,128)} %w_value.1, f32[3,3,256]{2,1,0:T(4,128)} %taps_in.1, f32[16,256]{1,0:T(8,128)} %bitcast.3, f32[16,256]{1,0:T(8,128)} %bitcast.4, ...), custom_call_target="tpu_custom_call" | custom-call | flops 12884901888 | bytes 4194304 | tf_op jit(solution)/shard_map/pallas_call | solution.py:409
  94.0 2.3 %copy.10 = bf16[1,128,4096]{2,1,0:T(8,128)(2,1)} copy(bf16[1,128,4096]{2,1,0:T(8,128)(2,1)} %shard_map.82) | data formatting | bytes 2097152

commit v5 on v4

--- a/solution.py
+++ b/solution.py
@@ -53,7 +53,7 @@
         return k, k1, v, v1, tuple(fade[r] * hs[r] + p for r in range(MODES))
 
     zero = jnp.zeros((SEGS, 128), jnp.float32)
-    *_, hs = lax.fori_loop(0, SPAN, first, (*before(1), *before(2), (zero,) * MODES), unroll=8)
+    *_, hs = lax.fori_loop(0, SPAN, first, (*before(1), *before(2), (zero,) * MODES), unroll=16)
     start = []
     for r in range(MODES):
         h = hs[r]
@@ -87,7 +87,7 @@
         if beside:
             carry = lax.fori_loop(4 * core, 4 * core + 4, stretch, carry)
         else:
-            carry = lax.fori_loop(core * (SPAN // 2), (core + 1) * (SPAN // 2), second, carry, unroll=8)
+            carry = lax.fori_loop(core * (SPAN // 2), (core + 1) * (SPAN // 2), second, carry, unroll=16)
         emit(core)
 
 

time: 96.4 us -> 96.1 us (level)
  no operation moved by 1% of the time
where the time goes in v5:
time: 96.1 us; the launch traced here: 96 us
  Pallas kernels  93.7 us (98%)
  local copies, waits for them, and re-layouts  2.29 us (2%)
    pallas_call x1, Pallas kernels, body(): pl.pallas_call(kernel, out_shape=jax.ShapeDtypeStruct((1, 128, 4096), jnp...  93.7 us
    unnamed x1, local copies, waits for them, and re-layouts  2.29 us

profile of v5, /device:TPU:1, one launch (start us, length us, event | category | flops | bytes accessed | tf_op | source)
XLA Modules:
  0.0 96.0 jit_solution(1430209885735199800)
XLA Ops:
  0.0 93.7 %shard_map.82 = bf16[1,128,4096]{2,1,0:T(8,128)(2,1)} custom-call(bf16[1,128,4096]{2,1,0:T(8,128)(2,1)} %tokens.1, f32[256,256]{1,0:T(8,128)} %w_query.1, f32[256,256]{1,0:T(8,128)} %w_key.1, f32[256,256]{1,0:T(8,128)} %w_value.1, f32[3,3,256]{2,1,0:T(4,128)} %taps_in.1, f32[16,256]{1,0:T(8,128)} %bitcast.3, f32[16,256]{1,0:T(8,128)} %bitcast.4, ...), custom_call_target="tpu_custom_call" | custom-call | flops 12884901888 | bytes 4194304 | tf_op jit(solution)/shard_map/pallas_call | solution.py:409
  93.7 2.3 %copy.10 = bf16[1,128,4096]{2,1,0:T(8,128)(2,1)} copy(bf16[1,128,4096]{2,1,0:T(8,128)(2,1)} %shard_map.82) | data formatting | bytes 2097152
